TPU v7x, 512 devices: a whole 4x8x8 slice. The times are simulated.
512 devices in a mesh: dp: 16 (over z, core), cent: 32 (over y, x).
Axes of the slice: x: 4, y: 8, z: 8, core: 2. Of those that a mesh axis runs over, the one named last changes fastest.
Arguments:
- embeddings: bfloat16 [12288, 1024], P(('dp', 'cent')), as said below
- outcomes: int32 [12288], P(('dp', 'cent')), may hold values 0 or 1
- seed_index: int32 [32768], P('cent'), may hold values from 0 to 12287
Outputs:
- centroids: bfloat16 [32768, 1024], P(('cent', 'dp'))
- step_scores: float32 [12288], P(('dp', 'cent'))
Inputs may be any that keep to these rules, and one draw needn't show every extreme that they name: `embeddings`: entries are bounded in magnitude by 44 / sqrt(1024).
All inputs are finite; a program needn't handle non-finite values. No bound on the sum of `outcomes` on one device may be relied on, other than what follows from the above.
Results may differ from a plain program's by a relative error of at most 0.01.
Values may be sent and summed in bfloat16 or wider, within the bound.
A program may use at most 64 MiB of HBM per device.

v0:
```python
import jax
import jax.numpy as jnp
from jax import lax
from jax.sharding import PartitionSpec as P

INVERSE_TEMP = 8.0
PSEUDO_COUNT = 1.0


def expect(row_block, labels, centroid_set):
    sq_norms = jnp.sum(jnp.square(centroid_set.astype(jnp.float32)), axis=1)
    products = lax.dot_general(
        row_block, centroid_set, (((1,), (1,)), ((), ())), preferred_element_type=jnp.float32
    )
    logits = INVERSE_TEMP * (products - 0.5 * sq_norms[None, :])
    local_max = jnp.max(logits, axis=1)
    row_max = lax.pmax(local_max, "cent")
    exponent = jnp.exp(logits - row_max[:, None])
    row_total = lax.psum(jnp.sum(exponent, axis=1), "cent")
    weights = exponent / row_total[:, None]
    rounded = weights.astype(jnp.bfloat16)
    masses = jnp.sum(rounded, axis=0, dtype=jnp.float32)
    successes = jnp.dot(labels, rounded, preferred_element_type=jnp.float32)
    masses, successes = lax.psum((masses, successes), "dp")
    return (weights, rounded, masses, successes)


def refresh(shares, old_part, mass_part):
    return (
        (shares + PSEUDO_COUNT * old_part.astype(jnp.float32)) / (mass_part + PSEUDO_COUNT)[:, None]
    ).astype(jnp.bfloat16)


def numerator_of(rounded, row_block):
    return lax.dot_general(
        rounded, row_block, (((0,), (0,)), ((), ())), preferred_element_type=jnp.float32
    )


def per_device(embeddings, outcomes, seed_index):
    rows_dev = embeddings.shape[0]
    feature_count = embeddings.shape[1]
    k_local = seed_index.shape[0]
    dp_size = lax.axis_size("dp")
    row_block, labels = (
        lax.all_gather(embeddings, "cent", axis=0, tiled=True),
        lax.all_gather(outcomes.astype(jnp.bfloat16), "cent", axis=0, tiled=True),
    )
    group_rows = row_block.shape[0]
    local_index = seed_index - lax.axis_index("dp") * group_rows
    present = (local_index >= 0) & (local_index < group_rows)
    picked_rows = jnp.take(row_block, jnp.clip(local_index, 0, group_rows - 1), axis=0)
    chosen = jnp.where(present[:, None], picked_rows.astype(jnp.float32), 0.0)
    centroid_set = lax.psum(chosen.astype(jnp.bfloat16), "dp")
    col_count = feature_count // dp_size
    row_count = k_local // dp_size
    weights, rounded, masses, successes = expect(row_block, labels, centroid_set)
    shares = lax.psum_scatter(
        numerator_of(rounded, row_block).astype(jnp.bfloat16), "dp", scatter_dimension=1, tiled=True
    ).astype(jnp.float32)
    offset = lax.axis_index("dp") * col_count
    old_part = lax.dynamic_slice_in_dim(centroid_set, offset, col_count, 1)
    updated = refresh(shares, old_part, masses)
    centroid_set = lax.all_gather(updated, "dp", axis=1, tiled=True)
    weights, rounded, masses, successes = expect(row_block, labels, centroid_set)
    final_shares = lax.psum_scatter(
        numerator_of(rounded, row_block).astype(jnp.bfloat16), "dp", scatter_dimension=0, tiled=True
    ).astype(jnp.float32)
    final_offset = lax.axis_index("dp") * row_count
    final_old = lax.dynamic_slice_in_dim(centroid_set, final_offset, row_count, 0)
    final_mass = lax.dynamic_slice_in_dim(masses, final_offset, row_count, 0)
    final_part = refresh(final_shares, final_old, final_mass)
    success_rate = (successes + 0.5 * PSEUDO_COUNT) / (masses + PSEUDO_COUNT)
    group_scores = lax.psum(jnp.dot(weights, success_rate, precision=lax.Precision.HIGHEST), "cent")
    own_scores = lax.dynamic_slice_in_dim(
        group_scores, lax.axis_index("cent") * rows_dev, rows_dev, 0
    )
    return (final_part, own_scores)


def solution(mesh):
    return jax.shard_map(
        per_device,
        mesh=mesh,
        in_specs=(P(("dp", "cent"), None), P(("dp", "cent")), P("cent")),
        out_specs=(P(("cent", "dp"), None), P(("dp", "cent"))),
        check_vma=False,
    )
```

profile of v0, /device:TPU:1, one launch (start us, length us, event | category | flops | bytes accessed | tf_op | source)
XLA Modules:
  0.0 824.0 jit_solution(8057888089337506268)
XLA Ops:
  9.3 85.4 %all-gather.3.cloned.1.call-done = bf16[768,1024]{1,0:T(8,128)(2,1)} async-done(((bf16[24,1024]{1,0:T(8,128)(2,1)}), bf16[768,1024]{1,0:T(8,128)(2,1)}) %all-gather.3.cloned.1.call-update) | async-done | bytes 1572880 | tf_op jit(solution)/shard_map/all_gather | solution.py:46
  94.8 6.6 gather_fusion
  101.4 2.6 copy.8
  103.9 3.5 select_convert_fusion
  107.6 123.0 %all-reduce.4.cloned.1.call-done = bf16[1024,1024]{0,1:T(8,128)(2,1)} async-done(((bf16[1024,1024]{0,1:T(8,128)(2,1)}), bf16[1024,1024]{0,1:T(8,128)(2,1)}) %all-reduce.4.cloned.1.call-update) | async-done | bytes 2097168 | tf_op jit(solution)/shard_map/psum | solution.py:54
  230.6 2.1 multiply_reduce_fusion.1
  232.7 5.2 fusion.2
  237.9 60.6 %pmax.14 = f32[768]{0:T(1024)S(1)} all-reduce(f32[768]{0:T(1024)S(1)} %get-tuple-element.14), channel_id=1, replica_groups=mesh['dp'=16,'cent'=32] {'cent'}, use_global_device_ids=true, to_apply=%region_3.4 | all-reduce | flops 768 | bytes 6144 | tf_op jit(solution)/shard_map/pmax | solution.py:17
  298.5 2.6 fusion.4
  301.0 55.7 %psum.50 = f32[768]{0:T(1024)S(1)} all-reduce(f32[768]{0:T(1024)S(1)} %fusion.4), channel_id=1, replica_groups=mesh['dp'=16,'cent'=32] {'cent'}, use_global_device_ids=true, to_apply=%region_5.6 | all-reduce | flops 768 | bytes 6144 | tf_op jit(solution)/shard_map/psum | solution.py:19
  356.8 2.8 convert_reduce_fusion
  359.6 3.2 convolution_convert_fusion.1
  362.9 51.8 %psum.51 = f32[1024]{0:T(1024)S(1)} all-reduce(f32[1024]{0:T(1024)S(1)} %get-tuple-element.10), channel_id=1, replica_groups=mesh['dp'=16,'cent'=32] {'dp'}, use_global_device_ids=true, to_apply=%region_8.9 | all-reduce | flops 1024 | bytes 8192 | tf_op jit(solution)/shard_map/psum | solution.py:24
  414.7 32.6 %reduce-scatter.5.cloned.1.call-done = bf16[1024,64]{0,1:T(8,128)(2,1)} async-done(((bf16[1024,1024]{0,1:T(8,128)(2,1)}), bf16[1024,64]{0,1:T(8,128)(2,1)}) %reduce-scatter.5.cloned.1.call-update) | async-done | bytes 131088 | tf_op jit(solution)/shard_map/reduce_scatter | solution.py:58
  447.4 1.7 divide_convert_fusion.2
  449.1 45.2 %all-gather.5.cloned.1.call-done = bf16[1024,1024]{0,1:T(8,128)(2,1)} async-done(((bf16[1024,64]{0,1:T(8,128)(2,1)}), bf16[1024,1024]{0,1:T(8,128)(2,1)}) %all-gather.5.cloned.1.call-update) | async-done | bytes 2097168 | tf_op jit(solution)/shard_map/all_gather | solution.py:64
  494.3 2.1 multiply_reduce_fusion
  496.4 5.2 fusion.3
  501.6 60.9 %pmax.15 = f32[768]{0:T(1024)S(1)} all-reduce(f32[768]{0:T(1024)S(1)} %get-tuple-element.16), channel_id=1, replica_groups=mesh['dp'=16,'cent'=32] {'cent'}, use_global_device_ids=true, to_apply=%region_11.12 | all-reduce | flops 768 | bytes 6144 | tf_op jit(solution)/shard_map/pmax | solution.py:17
  562.5 2.6 fusion.5
  565.1 56.2 %psum.52 = f32[768]{0:T(1024)S(1)} all-reduce(f32[768]{0:T(1024)S(1)} %fusion.5), channel_id=1, replica_groups=mesh['dp'=16,'cent'=32] {'cent'}, use_global_device_ids=true, to_apply=%region_13.14 | all-reduce | flops 768 | bytes 6144 | tf_op jit(solution)/shard_map/psum | solution.py:19
  621.3 2.8 convert_reduce_fusion.1
  624.1 1.7 copy-done.1
  625.8 3.2 fusion.17
  629.0 1.4 dynamic-slice
  631.4 56.9 %all-reduce = bf16[768]{0:T(1024)(128)(2,1)S(1)} all-reduce(bf16[768]{0:T(1024)(128)(2,1)S(1)} %dynamic-update-slice), channel_id=1, replica_groups=mesh['dp'=16,'cent'=32] {'cent'}, use_global_device_ids=true, to_apply=%add | all-reduce | flops 768 | bytes 3072
  688.3 2.4 fusion.15
  690.6 65.7 %all-reduce.1 = (f32[1024]{0:T(1024)S(1)}, f32[1024]{0:T(1024)S(1)}) all-reduce(f32[1024]{0:T(1024)S(1)} %get-tuple-element.8, f32[1024]{0:T(1024)S(1)} %bitcast.42), channel_id=1, replica_groups=mesh['dp'=16,'cent'=32] {'dp'}, use_global_device_ids=true, to_apply=%region_16.17 | all-reduce | flops 2048 | bytes 16384 | tf_op jit(solution)/shard_map/psum | solution.py:24
  756.4 1.7 fusion.7
  758.1 55.7 %psum.55 = f32[768]{0:T(1024)S(1)} all-reduce(f32[768]{0:T(1024)S(1)} %fusion.7), channel_id=1, replica_groups=mesh['dp'=16,'cent'=32] {'cent'}, use_global_device_ids=true, to_apply=%region_18.19 | all-reduce | flops 768 | bytes 6144 | tf_op jit(solution)/shard_map/psum | solution.py:74
  814.5 1.1 copy.12
  815.6 1.1 divide_convert_fusion.1
  (31 shorter events, 4.1 us)
Async XLA Ops:
  7.2 87.6 %all-gather.3.cloned.1.call-start = ((), (), s32[]{:S(2)}) async-start(), calls=%async_computation.2 | async-start | bytes 1622016 | tf_op jit(solution)/shard_map/all_gather | solution.py:46
  7.9 222.7 %all-reduce.4.cloned.1.call-start = ((), (), s32[]{:S(2)}) async-start(), calls=%async_computation.3 | async-start | bytes 4194304 | tf_op jit(solution)/shard_map/psum | solution.py:54
  107.5 125.2 %copy-start = (bf16[768,1024]{1,0:T(8,128)(2,1)S(1)}, bf16[768,1024]{1,0:T(8,128)(2,1)}, u32[]{:S(2)}) copy-start(bf16[768,1024]{1,0:T(8,128)(2,1)} %all-gather.3.cloned.1.call-done) | copy-start | bytes 4718596
  107.5 339.9 %reduce-scatter.5.cloned.1.call-start = ((), (), s32[]{:S(2)}) async-start(), calls=%async_computation.4 | async-start | bytes 2228224 | tf_op jit(solution)/shard_map/reduce_scatter | solution.py:58
  362.9 131.4 %all-gather.5.cloned.1.call-start = ((), (), s32[]{:S(2)}) async-start(), calls=%async_computation.5 | async-start | bytes 2228224 | tf_op jit(solution)/shard_map/all_gather | solution.py:64
  449.1 365.4 %reduce-scatter.7.cloned.1.call-start = ((), (), s32[]{:S(2)}) async-start(), calls=%async_computation.6 | async-start | bytes 2228224
  624.1 1.7 copy-start.1
  625.8 3.2 copy-start.3
  629.0 127.4 %copy-start.2 = (f32[1024,768]{1,0:T(8,128)S(1)}, f32[1024,768]{1,0:T(8,128)}, u32[]{:S(2)}) copy-start(f32[1024,768]{1,0:T(8,128)} %copy-done.1) | copy-start | bytes 9437188
Sparse Core Ops, SparseCore 0:
  11.2 83.5 all-gather.2
  107.6 122.8 all-reduce.3
  363.0 84.3 reduce-scatter.4
  449.9 44.3 all-gather.4
  629.1 81.9 reduce-scatter.6
where the time goes:
time: 838 us; the launch traced here: 824 us
  blocking collectives  464 us (55%)
  waiting for transfers between devices  287 us (34%)
  other arithmetic  22.7 us (3%)
  matrix products  21 us (3%)
  local copies, waits for them, and re-layouts  14.9 us (2%)
  between operations  14.6 us (2%)
    psum x1, waiting for transfers between devices, per_device(): centroid_set = lax.psum(chosen.astype(jnp.bfloat16), 'dp')  123 us
    pmax x2, blocking collectives, expect(): row_max = lax.pmax(local_max, 'cent')  121 us
    psum x2, blocking collectives, expect(): masses, successes = lax.psum((masses, successes), 'dp')  117 us
    psum x2, blocking collectives, expect(): row_total = lax.psum(jnp.sum(exponent, axis=1), 'cent')  112 us
    all_gather x1, waiting for transfers between devices, per_device(): lax.all_gather(embeddings, 'cent', axis=0, tiled=True)  85.4 us
    unnamed x1, blocking collectives  56.9 us
    psum x1, blocking collectives, per_device(): lax.psum(jnp.dot(weights, success_rate, precision=lax.Precision.HIGHEST),...  55.7 us
    all_gather x1, waiting for transfers between devices, per_device(): centroid_set = lax.all_gather(updated, 'dp', axis=1, tiled=True)  45.2 us
  transfers between devices with their start and end apart: 5, of which 4 were waited for; matrix products, arithmetic and copies ran while one was open for 1% of the time, Pallas kernels for 0%

commit v1 on v0

v1 whole, which is shorter than its diff:
```python
import functools

import jax
import jax.numpy as jnp
from jax import lax
from jax.experimental import pallas as pl
from jax.experimental.pallas import tpu as pltpu
from jax.sharding import PartitionSpec as P

INVERSE_TEMP = 8.0
PSEUDO_COUNT = 1.0
ABSENT = -1e30
MESH = pl.DeviceIdType.MESH
F32 = jnp.float32
BF16 = jnp.bfloat16


class Sizes:
    def __init__(self, z, y, x, rows, features, seeds):
        self.z, self.y, self.x = z, y, x
        self.rows = rows
        self.chip = 2 * rows
        self.features = features
        self.half = features // 2
        self.slab = features // z
        self.local = (z // 2) * self.chip
        self.group = y * x * self.chip
        self.blocks = 4 if y >= 4 else 1
        self.width = self.group // self.blocks
        self.seeds = seeds
        self.outs = seeds // (2 * z)
        self.lanes = -(-self.local // 128) * 128


def scratch_of(s):
    dma = pltpu.SemaphoreType.DMA
    v = pltpu.VMEM
    return dict(
        mine=v((32, s.features), BF16),
        theirs=v((32, s.features), BF16),
        block=v((s.chip, s.features), BF16),
        rows=v((s.y, s.x, s.chip, s.features), BF16),
        cents=v((2, s.local, s.features), BF16),
        lab_x=v((2, s.x, 1, s.width), F32),
        lab_s=v((1, s.width), F32),
        lab_y=v((s.y, 1, s.width), F32),
        cnt_s=v((s.x, s.y, s.lanes), F32),
        cnt_x=v((s.x, s.y, s.lanes), F32),
        cnt_t=v((s.y, 1, s.lanes), F32),
        cnt_y=v((s.y, 1, s.lanes), F32),
        logits=v((s.blocks, s.local, s.width), F32),
        probs=v((s.blocks, s.local, s.width), BF16),
        st_s=v((3, s.blocks, 1, s.width), F32),
        st_x=v((3, 2, s.x, s.blocks, 1, s.width), F32),
        st_t=v((3, s.blocks, 1, s.width), F32),
        st_y=v((3, s.y, s.blocks, 1, s.width), F32),
        mw_s=v((2, 8, s.lanes), F32),
        mw_r=v((2, s.z, 8, s.lanes), F32),
        num_s=v((2, s.z, s.local, s.slab), BF16),
        num_r=v((2, s.z, s.local, s.slab), BF16),
        table=v((2, s.y, s.x, s.local, s.slab), BF16),
        wide=v((2 * s.y * s.x * s.local, s.slab), F32),
        picked=v((s.outs, s.slab), F32),
        out_s=v((s.z, s.outs, s.slab), BF16),
        out_r=v((s.z, s.outs, s.slab), BF16),
        core_sem=dma((2, 3)),
        a1_sem=dma((2, 2, s.x)),
        a2_sem=dma((2, 2, s.y)),
        b1_sem=dma((2, 2, s.y)),
        b2_sem=dma((2, 2, s.x)),
        cent_sem=dma((2, s.z)),
        lab_sem=dma((2, 2 * s.x)),
        laby_sem=dma((2, s.y)),
        cnt_sem=dma((2, s.x)),
        cnty_sem=dma((2, s.y)),
        stx_sem=dma((3, 2, 2 * s.x)),
        sty_sem=dma((3, 2, s.y)),
        mw_sem=dma((2, 2, s.z)),
        num_sem=dma((2, 2, s.z)),
        new_sem=dma((2, s.z)),
        out_sem=dma((2, s.z)),
    )


def kernel(s, names, emb, lab, qr, pos, out_c, out_v, *scratch):
    ref = dict(zip(names, scratch))
    dp, cent = lax.axis_index("dp"), lax.axis_index("cent")
    z, core = dp // 2, dp % 2
    y, x = cent // s.x, cent % s.x

    def device(z_, core_, y_, x_):
        return (z_ * 2 + core_, y_ * s.x + x_)

    to_z = lambda p: device(p, core, y, x)
    to_y = lambda p: device(z, core, p, x)
    to_x = lambda p: device(z, core, y, p)
    to_cx = lambda p: device(z, p // s.x, y, p % s.x)
    partner = device(z, 1 - core, y, x)
    cx = core * s.x + x

    def each(n, me, do):
        def step(i, carry):
            do(lax.rem(me + i, n))
            return carry

        lax.fori_loop(1, n, step, 0)

    def copy(src, dst, sems, out_index, in_index, to):
        return pltpu.make_async_remote_copy(
            src_ref=src,
            dst_ref=dst,
            send_sem=sems.at[0, out_index],
            recv_sem=sems.at[1, in_index],
            device_id=to,
            device_id_type=MESH,
        )

    pending = []

    class Exchange:
        def __init__(self, n, me, to, sems, src, dst):
            self.n, self.me, self.to, self.sems, self.src, self.dst = n, me, to, sems, src, dst

        def start(self):
            each(self.n, self.me, lambda p: copy(
                self.src(p), self.dst(self.me), self.sems, p, self.me, self.to(p)).start())
            pending.append(self)

        def arrived(self):
            each(self.n, self.me, lambda p: copy(
                self.src(p), self.dst(p), self.sems, p, p, self.to(p)).wait_recv())

        def sent(self):
            each(self.n, self.me, lambda p: copy(
                self.src(p), self.dst(self.me), self.sems, p, self.me, self.to(p)).wait_send())

    barrier = pltpu.get_barrier_semaphore()

    def greet(to):
        return lambda p: pl.semaphore_signal(barrier, inc=1, device_id=to(p), device_id_type=MESH)

    each(2 * s.x, cx, greet(to_cx))
    each(s.y, y, greet(to_y))
    each(s.z, z, greet(to_z))
    pl.semaphore_wait(barrier, 2 * s.x - 1 + s.y - 1 + s.z - 1)

    mine, theirs = ref["mine"], ref["theirs"]
    mine[...] = jnp.concatenate(
        [emb[...].astype(F32), jnp.zeros((32 - s.rows, s.features), F32)], axis=0
    ).astype(BF16)
    swap = pltpu.make_async_remote_copy(
        src_ref=mine, dst_ref=theirs, send_sem=ref["core_sem"].at[0, 0],
        recv_sem=ref["core_sem"].at[1, 0], device_id=partner, device_id_type=MESH,
    )
    swap.start()

    lab_x = ref["lab_x"]
    lab_x[core, x] = lab[...]
    lab_ex = Exchange(2 * s.x, cx, to_cx, ref["lab_sem"],
                      lambda p: lab_x.at[core, x], lambda p: lab_x.at[p // s.x, p % s.x])
    lab_ex.start()

    cnt_s, cnt_x = ref["cnt_s"], ref["cnt_x"]
    places = lax.broadcasted_iota(jnp.int32, (s.lanes, s.seeds), 0)
    hot_r = jnp.where(places == qr[1:2, :], 1.0, 0.0).astype(BF16)
    for xx in range(s.x):
        owner = lax.broadcasted_iota(jnp.int32, (s.y, s.seeds), 0) * s.x + (xx + core * s.x * s.y)
        hot_q = jnp.where(owner == qr[0:1, :], 1.0, 0.0).astype(BF16)
        cnt_s[xx] = lax.dot_general(hot_q, hot_r, (((1,), (1,)), ((), ())), preferred_element_type=F32)
    cnt_ex = Exchange(s.x, x, to_x, ref["cnt_sem"], lambda p: cnt_s.at[p], lambda p: cnt_x.at[p])
    cnt_ex.start()

    swap.wait_recv()
    own = mine[...].astype(F32)[: s.rows]
    other = theirs[...].astype(F32)[: s.rows]
    rows, block = ref["rows"], ref["block"]
    first = jnp.where(core == 0, own, other)
    second = jnp.where(core == 0, other, own)
    block[...] = jnp.concatenate([first, second], axis=0).astype(BF16)

    def plane(t, at, tall, low, forward_from, forward_to):
        top, rest = pl.ds(0, low), pl.ds(low, tall - low)
        a1 = Exchange(s.x, x, to_x, ref["a1_sem"].at[t], lambda p: at(y, x, top), lambda p: at(y, p, top))
        b1 = Exchange(s.y, y, to_y, ref["b1_sem"].at[t], lambda p: at(y, x, rest), lambda p: at(p, x, rest))
        every = slice(None)
        a2 = Exchange(s.y, y, to_y, ref["a2_sem"].at[t], lambda p: at(y, every, top), lambda p: at(p, every, top))
        b2 = Exchange(s.x, x, to_x, ref["b2_sem"].at[t], lambda p: at(every, x, rest), lambda p: at(every, p, rest))
        a1.start()
        b1.start()
        yield
        a1.arrived()
        a2.start()
        b1.arrived()
        b2.start()
        yield
        a2.arrived()
        b2.arrived()
        share = pltpu.make_async_remote_copy(
            src_ref=forward_from, dst_ref=forward_from, send_sem=ref["core_sem"].at[0, 1 + t],
            recv_sem=ref["core_sem"].at[1, 1 + t], device_id=partner, device_id_type=MESH,
        )
        share.start()
        yield
        pltpu.make_async_remote_copy(
            src_ref=forward_from, dst_ref=forward_to, send_sem=ref["core_sem"].at[0, 1 + t],
            recv_sem=ref["core_sem"].at[1, 1 + t], device_id=partner, device_id_type=MESH,
        ).wait_recv()
        share.wait_send()

    def lanes_of(c):
        return pl.ds(pl.multiple_of(c * s.half, 128), s.half)

    rows[y, x, :, lanes_of(core)] = block[:, lanes_of(core)]
    gather = plane(
        0,
        lambda yy, xx, part: rows.at[yy, xx, part, lanes_of(core)],
        s.chip,
        16,
        rows.at[:, :, :, lanes_of(core)],
        rows.at[:, :, :, lanes_of(1 - core)],
    )
    next(gather)

    cents = ref["cents"]
    zh = s.z // 2

    def cent_copy(src_z, to):
        place = pl.ds(pl.multiple_of((src_z % zh) * s.chip, 16), s.chip)
        return copy(block, cents.at[0, place, :], ref["cent_sem"], to, src_z, to_z(to))

    @pl.when(z // zh == core)
    def _():
        each(s.z, z, lambda p: cent_copy(z, p).start())
        cents[0, pl.ds(pl.multiple_of((z % zh) * s.chip, 16), s.chip), :] = block[...]

    cnt_ex.arrived()
    cnt_x[x] = cnt_s[x]
    total = cnt_x[0]
    for xx in range(1, s.x):
        total = total + cnt_x[xx]
    cnt_t, cnt_y = ref["cnt_t"], ref["cnt_y"]
    for yy in range(s.y):
        cnt_t[yy] = total[yy : yy + 1]
    cnty_ex = Exchange(s.y, y, to_y, ref["cnty_sem"], lambda p: cnt_t.at[p], lambda p: cnt_y.at[p])
    cnty_ex.start()
    lab_ex.arrived()
    lab_s, lab_y = ref["lab_s"], ref["lab_y"]
    line = lab_x[0, 0]
    for i in range(1, 2 * s.x):
        line = line + lab_x[i // s.x, i % s.x]
    lab_y[y] = line
    laby_ex = Exchange(s.y, y, to_y, ref["laby_sem"], lambda p: lab_y.at[y], lambda p: lab_y.at[p])
    laby_ex.start()

    next(gather)

    def to_column(row):
        eye = lax.broadcasted_iota(jnp.int32, (s.local, s.lanes), 0) == lax.broadcasted_iota(
            jnp.int32, (s.local, s.lanes), 1
        )
        return jnp.sum(jnp.where(eye, row, 0.0), axis=1, keepdims=True)

    cnty_ex.arrived()
    cnt_y[y] = cnt_t[y]
    line = cnt_y[0]
    for yy in range(1, s.y):
        line = line + cnt_y[yy]
    weight = to_column(line)
    laby_ex.arrived()

    @pl.when(z // zh == core)
    def _():
        each(s.z, z, lambda p: cent_copy(z, p).wait_send())

    def cents_in(i, carry):
        src_z = core * zh + i

        @pl.when(src_z != z)
        def _():
            place = pl.ds(pl.multiple_of(i * s.chip, 16), s.chip)
            copy(block, cents.at[0, place, :], ref["cent_sem"], src_z, src_z, to_z(src_z)).wait_recv()

        return carry

    lax.fori_loop(0, zh, cents_in, 0)
    next(gather)
    for _ in gather:
        pass

    def rows_of(b, lanes):
        per = s.y // s.blocks
        return rows[pl.ds(b * per, per), :, :, lanes].reshape(s.width, -1)

    logits, probs = ref["logits"], ref["probs"]
    everything = slice(None)

    def blocks(do):
        def step(b, carry):
            do(b)
            return carry

        lax.fori_loop(0, s.blocks, step, 0)

    def lse_of(parts):
        top = functools.reduce(jnp.maximum, parts)
        return top + jnp.log(sum(jnp.exp(part - top) for part in parts))

    def total_of(parts):
        return sum(parts)

    def all_reduce(t, combine):
        st_s, st_x, st_t, st_y = (ref[name].at[t] for name in ("st_s", "st_x", "st_t", "st_y"))
        near = Exchange(2 * s.x, cx, to_cx, ref["stx_sem"].at[t], lambda p: st_s, lambda p: st_x.at[p // s.x, p % s.x])
        far = Exchange(s.y, y, to_y, ref["sty_sem"].at[t], lambda p: st_t, lambda p: st_y.at[p])
        near.start()
        yield
        near.arrived()
        st_x[core, x] = st_s[...]
        st_t[...] = combine([st_x[i // s.x, i % s.x] for i in range(2 * s.x)])
        far.start()
        yield
        far.arrived()
        st_y[y] = st_t[...]
        st_s_final[t][...] = combine([st_y[i] for i in range(s.y)])

    st_s_final = [ref["st_x"].at[t, 0, 0] for t in range(3)]

    for t in range(2):
        held = cents.at[t]
        wide = held[...].astype(F32)
        norm = jnp.sum(wide * wide, axis=1, keepdims=True)
        bias = jnp.where(weight > 0.0, (-0.5 * INVERSE_TEMP) * norm, ABSENT)
        st_s = ref["st_s"].at[t]

        def scores_of(b):
            product = lax.dot_general(
                held[...], rows_of(b, everything), (((1,), (1,)), ((), ())), preferred_element_type=F32
            )
            value = INVERSE_TEMP * product + bias
            value = jnp.where(weight > 0.0, value, ABSENT)
            logits[b] = value
            top = jnp.max(value, axis=0, keepdims=True)
            mass = jnp.sum(weight * jnp.exp(value - top), axis=0, keepdims=True)
            st_s[b] = jnp.maximum(top + jnp.log(mass), ABSENT)

        blocks(scores_of)
        for _ in all_reduce(t, lse_of):
            pass
        norm_of = st_s_final[t]
        mw_s, mw_r = ref["mw_s"].at[t], ref["mw_r"].at[t]
        mw_s[...] = jnp.zeros_like(mw_s)

        def shares_of(b):
            value = jnp.exp(logits[b] - norm_of[b])
            if t == 1:
                logits[b] = value
            rounded = value.astype(BF16)
            probs[b] = rounded
            per = s.y // s.blocks
            label = lab_y[b * per]
            for i in range(1, per):
                label = label + lab_y[b * per + i]
            line = lax.broadcasted_iota(jnp.int32, (8, s.width), 0)
            left = jnp.where(line == 0, 1.0, jnp.where(line == 1, label, 0.0)).astype(BF16)
            both = lax.dot_general(left, rounded, (((1,), (1,)), ((), ())), preferred_element_type=F32)
            mw_s[:, : s.local] += both

        blocks(shares_of)
        mw_ex = Exchange(s.z, z, to_z, ref["mw_sem"].at[t], lambda p: mw_s, lambda p: mw_r.at[p])
        mw_ex.start()

        num_s, num_r = ref["num_s"].at[t], ref["num_r"].at[t]
        num_ex = Exchange(s.z, z, to_z, ref["num_sem"].at[t], lambda p: num_s.at[p], lambda p: num_r.at[p])
        pairs = s.z // 2

        def numer_of(i, carry):
            pair = lax.rem(z // 2 + 1 + i, pairs)
            lanes = pl.ds(pl.multiple_of(pair * 2 * s.slab, 128), 2 * s.slab)
            acc = jnp.zeros((s.local, 2 * s.slab), F32)
            for b in range(s.blocks):
                acc = acc + jnp.dot(probs[b], rows_of(b, lanes), preferred_element_type=F32)
            for side in range(2):
                p = pair * 2 + side
                num_s[p] = acc[:, side * s.slab : (side + 1) * s.slab].astype(BF16)

                @pl.when(p != z)
                def _():
                    copy(num_s.at[p], num_r.at[z], ref["num_sem"].at[t], p, z, to_z(p)).start()

            return carry

        lax.fori_loop(0, pairs, numer_of, 0)
        pending.append(num_ex)
        mw_ex.arrived()
        mw_r[z] = mw_s[...]
        both = mw_r[0]
        for i in range(1, s.z):
            both = both + mw_r[i]
        mass = to_column(both[0:1])
        if t == 1:
            wins = to_column(both[1:2])
            rate = weight * ((wins + 0.5 * PSEUDO_COUNT) / (mass + PSEUDO_COUNT))
            sc = ref["st_s"].at[2]

            def step_scores(b):
                sc[b] = jnp.sum(logits[b] * rate, axis=0, keepdims=True)

            blocks(step_scores)
            reduce_scores = all_reduce(2, total_of)
            next(reduce_scores)
        num_ex.arrived()
        num_r[z] = num_s[z]
        mylanes = pl.ds(pl.multiple_of(z * s.slab, 128), s.slab)
        acc = num_r[0].astype(F32)
        for i in range(1, s.z):
            acc = acc + num_r[i].astype(F32)
        acc = acc + PSEUDO_COUNT * held[:, mylanes].astype(F32)
        fresh = (acc / (mass + PSEUDO_COUNT)).astype(BF16)
        if t == 0:
            cents[1, :, mylanes] = fresh

            def slab_at(p):
                return cents.at[1, :, pl.ds(pl.multiple_of(p * s.slab, 128), s.slab)]

            new_ex = Exchange(s.z, z, to_z, ref["new_sem"], lambda p: slab_at(z), slab_at)
            new_ex.start()
            new_ex.arrived()

    table, wide = ref["table"], ref["wide"]
    table[core, y, x] = fresh
    gather = plane(
        1,
        lambda yy, xx, part: table.at[core, yy, xx, part, :],
        s.local,
        s.local // 3,
        table.at[core],
        table.at[1 - core],
    )
    next(gather)
    next(reduce_scores)
    next(gather)
    for _ in reduce_scores:
        pass
    final = st_s_final[2]
    offset = cent * s.chip + core * s.rows
    n_out = 32
    column = jnp.zeros((n_out, 1), F32)
    for b in range(s.blocks):
        here = lax.broadcasted_iota(jnp.int32, (n_out, s.width), 1) + b * s.width
        wanted = lax.broadcasted_iota(jnp.int32, (n_out, s.width), 0) + offset
        column = column + jnp.sum(jnp.where(here == wanted, final[b], 0.0), axis=1, keepdims=True)
    eye = lax.broadcasted_iota(jnp.int32, (n_out, 128), 0) == lax.broadcasted_iota(jnp.int32, (n_out, 128), 1)
    out_v[...] = jnp.sum(jnp.where(eye, column, 0.0), axis=0, keepdims=True)

    next(gather)
    for _ in gather:
        pass

    def widen(i, carry):
        a, yy = i // s.y, i % s.y
        size = s.x * s.local
        wide[pl.ds(pl.multiple_of(i * size, 16), size), :] = (
            table[a, yy].reshape(size, s.slab).astype(F32)
        )
        return carry

    lax.fori_loop(0, 2 * s.y, widen, 0)
    picked, out_s, out_r = ref["picked"], ref["out_s"], ref["out_r"]
    out_ex = Exchange(s.z, z, to_z, ref["out_sem"], lambda p: out_s.at[p], lambda p: out_r.at[p])

    def pick(i, carry):
        p = lax.rem(z + 1 + i, s.z)
        base = (2 * p + core) * s.outs

        def eight(j, carry):
            for k in range(8):
                n = j * 8 + k
                picked[pl.ds(n, 1), :] = wide[pl.ds(pos[base + n], 1), :]
            return carry

        lax.fori_loop(0, s.outs // 8, eight, 0)
        out_s[p] = picked[...].astype(BF16)

        @pl.when(p != z)
        def _():
            copy(out_s.at[p], out_r.at[z], ref["out_sem"], p, z, to_z(p)).start()

        return carry

    lax.fori_loop(0, s.z, pick, 0)
    pending.append(out_ex)
    out_ex.arrived()
    out_r[z] = out_s[z]
    for i in range(s.z):
        out_c[:, i * s.slab : (i + 1) * s.slab] = out_r[i]
    swap.wait_send()
    for exchange in pending:
        exchange.sent()


def per_device(s, embeddings, outcomes, seed_index):
    core = lax.axis_index("dp") % 2
    cent = lax.axis_index("cent")
    plane = s.rows * s.x * s.y
    dp, rest = seed_index // plane, seed_index % plane
    zs, side = dp // 2, dp % 2
    zh = s.z // 2
    q = (zs // zh) * (s.x * s.y) + rest // s.rows
    r = (zs % zh) * s.chip + side * s.rows + rest % s.rows
    qr = jnp.stack([q, r])
    pos = q * s.local + r
    offset = (cent * s.chip) % s.width + core * s.rows
    spot = lax.broadcasted_iota(jnp.int32, (s.rows, s.width), 1) - lax.broadcasted_iota(
        jnp.int32, (s.rows, s.width), 0
    )
    lab = jnp.sum(
        jnp.where(spot == offset, outcomes.astype(F32)[:, None], 0.0), axis=0, keepdims=True
    )
    scratch = scratch_of(s)
    vmem = pl.BlockSpec(memory_space=pltpu.VMEM)
    out_c, out_v = pl.pallas_call(
        functools.partial(kernel, s, tuple(scratch)),
        out_shape=(
            jax.ShapeDtypeStruct((s.outs, s.features), BF16),
            jax.ShapeDtypeStruct((1, 128), F32),
        ),
        in_specs=[vmem, vmem, vmem, pl.BlockSpec(memory_space=pltpu.SMEM)],
        out_specs=(vmem, vmem),
        scratch_shapes=list(scratch.values()),
        compiler_params=pltpu.CompilerParams(
            collective_id=0, has_side_effects=True, vmem_limit_bytes=48 * 1024 * 1024
        ),
    )(embeddings, lab, qr, pos)
    return out_c, out_v[0, : s.rows]


def build(mesh, y, x):
    z = mesh.shape["dp"] // 2

    def run(embeddings, outcomes, seed_index):
        devices = mesh.shape["dp"] * mesh.shape["cent"]
        s = Sizes(
            z, y, x, embeddings.shape[0] // devices, embeddings.shape[1],
            seed_index.shape[0] // mesh.shape["cent"],
        )
        return jax.shard_map(
            functools.partial(per_device, s),
            mesh=mesh,
            in_specs=(P(("dp", "cent"), None), P(("dp", "cent")), P("cent")),
            out_specs=(P(("cent", "dp"), None), P(("dp", "cent"))),
            check_vma=False,
        )(embeddings, outcomes, seed_index)

    return run


def solution(mesh):
    return build(mesh, mesh.shape["cent"] // 4, 4)
```

time: 838 us -> 138 us (0.16); the launches traced: 824 us -> 138 us
  blocking collectives: 464 us -> 0 us
  waiting for transfers between devices: 287 us -> 0 us
  Pallas kernels: 0 us -> 135 us
  other arithmetic: 22.7 us -> 0.14 us
  matrix products: 21 us -> 0 us
  between operations: 14.6 us -> 0.7 us
  local copies, waits for them, and re-layouts: 14.9 us -> 2.38 us
    psum x5 -> x0, blocking collectives: 285 us -> none  [the longest x2 117 us: expect(): masses, successes = lax.psum((masses, successes), 'dp')]
    pallas_call x0 -> x1, Pallas kernels: none -> 135 us  [per_device(): pl.pallas_call(functools.partial(kernel, s, tuple(scratch)), out_shape=(j...]
    all_gather x2 -> x0, waiting for transfers between devices: 131 us -> none  [the longest x1 85.4 us: per_device(): lax.all_gather(embeddings, 'cent', axis=0, tiled=True)]
    psum x1 -> x0, waiting for transfers between devices: 123 us -> none  [per_device(): centroid_set = lax.psum(chosen.astype(jnp.bfloat16), 'dp')]
    pmax x2 -> x0, blocking collectives: 121 us -> none  [expect(): row_max = lax.pmax(local_max, 'cent')]
    unnamed x1 -> x0, blocking collectives: 56.9 us -> none
    reduce_scatter x1 -> x0, waiting for transfers between devices: 32.6 us -> none  [per_device(): lax.psum_scatter(numerator_of(rounded, row_block).astype(jnp.bfloat16), '...]
    dot_general x6 -> x0, matrix products: 21 us -> none  [the longest x2 10.4 us: expect(): lax.dot_general(row_block, centroid_set, (((1,), (1,)), ((), ())), prefer...]
  transfers between devices with their start and end apart: 5 -> 0, of which waited for: 4 -> 0; matrix products, arithmetic and copies ran while one was open for 1% -> 0% of each run, Pallas kernels for 0% -> 0%
where the time goes in v1:
time: 138 us
  Pallas kernels  135 us (98%)
  local copies, waits for them, and re-layouts  2.38 us (2%)
    pallas_call x1, Pallas kernels, per_device(): pl.pallas_call(functools.partial(kernel, s, tuple(scratch)), out_shape=(j...  135 us

profile of v1, /device:TPU:1, one launch (start us, length us, event | category | flops | bytes accessed | tf_op | source)
XLA Modules:
  0.0 138.1 jit_solution(8373968649421171903)
XLA Ops:
  0.6 0.0 copy-start.2
  0.6 0.0 copy-start
  0.7 0.6 copy-done.2
  1.3 0.0 copy-start.1
  1.3 0.1 select_reduce_fusion
  1.4 0.6 copy-done.1
  2.0 0.0 copy-done
  2.0 134.9 %shard_map.50 = (bf16[64,1024]{1,0:T(8,128)(2,1)S(1)}, f32[1,128]{1,0:T(1,128)S(1)}) custom-call(bf16[24,1024]{1,0:T(8,128)(2,1)S(1)} %copy-done, f32[1,384]{1,0:T(1,128)S(1)} %broadcast_in_dim.18.lab, s32[2,1024]{1,0:T(2,128)S(1)} %pad_add_fusion.qr, s32[1024]{0:T(1024)S(1)} %get-tuple-element.6.pos), custom_call_target="tpu_custom_call" | custom-call | tf_op jit(solution)/shard_map/pallas_call | solution.py:521
  136.9 0.5 slice_bitcast_fusion
  137.5 0.7 copy.6
  (4 shorter events, 0.1 us)
Async XLA Ops:
  0.6 0.7 copy-start.2
  0.6 1.4 %copy-start = (bf16[24,1024]{1,0:T(8,128)(2,1)S(1)}, bf16[24,1024]{1,0:T(8,128)(2,1)}, u32[]{:S(2)}) copy-start(bf16[24,1024]{1,0:T(8,128)(2,1)} %emb.1) | copy-start | bytes 147460
  1.3 0.7 copy-start.1

commit v2 on v1

v2 whole, which is shorter than its diff:
```python
import functools

import jax
import jax.numpy as jnp
from jax import lax
from jax.experimental import pallas as pl
from jax.experimental.pallas import tpu as pltpu
from jax.sharding import PartitionSpec as P

INVERSE_TEMP = 8.0
PSEUDO_COUNT = 1.0
ABSENT = -1e30
MESH = pl.DeviceIdType.MESH
F32 = jnp.float32
BF16 = jnp.bfloat16


class Sizes:
    def __init__(self, z, y, x, rows, features, seeds):
        self.z, self.y, self.x = z, y, x
        self.rows = rows
        self.chip = 2 * rows
        self.features = features
        self.half = features // 2
        self.slab = features // z
        self.local = (z // 2) * self.chip
        self.group = y * x * self.chip
        self.width = x * self.chip
        self.span = -(-self.width // 128) * 128
        self.seeds = seeds
        self.outs = seeds // (2 * z)
        self.lanes = -(-self.local // 128) * 128


def scratch_of(s):
    dma = pltpu.SemaphoreType.DMA
    v = pltpu.VMEM
    return dict(
        mine=v((32, s.features), BF16),
        theirs=v((32, s.features), BF16),
        block=v((s.chip, s.features), BF16),
        rows=v((s.y, s.x, s.chip, s.features), BF16),
        cents=v((2, s.local, s.features), BF16),
        lab_x=v((2, s.x, 1, s.span), F32),
        lab_y=v((s.y, 1, s.span), F32),
        cnt_s=v((s.x, s.y, s.lanes), F32),
        cnt_x=v((s.x, s.y, s.lanes), F32),
        cnt_t=v((s.y, 1, s.lanes), F32),
        cnt_y=v((s.y, 1, s.lanes), F32),
        logits=v((s.y, s.local, s.width), F32),
        probs=v((s.y, s.local, s.width), BF16),
        st_s=v((3, s.y, 1, s.span), F32),
        st_x=v((3, 2, s.x, s.y, 1, s.span), F32),
        st_t=v((3, s.y, 1, s.span), F32),
        st_y=v((3, s.y, s.y, 1, s.span), F32),
        st_f=v((3, s.y, 1, s.span), F32),
        mw_s=v((2, 8, s.lanes), F32),
        mw_r=v((2, s.z, 8, s.lanes), F32),
        num_s=v((2, s.z, s.local, s.slab), BF16),
        num_r=v((2, s.z, s.local, s.slab), BF16),
        table=v((2, s.y, s.x, s.local, s.slab), BF16),
        wide=v((2 * s.y * s.x * s.local, s.slab), F32),
        picked=v((s.outs, s.slab), F32),
        out_s=v((s.z, s.outs, s.slab), BF16),
        out_r=v((s.z, s.outs, s.slab), BF16),
        core_sem=dma((2,)),
        share_sem=dma((2, 2, s.y)),
        a1_sem=dma((2, 2, s.x)),
        a2_sem=dma((2, 2, s.y)),
        b1_sem=dma((2, 2, 2 * s.y)),
        b2_sem=dma((2, 2, 2 * s.y * s.x)),
        cent_sem=dma((2, s.z)),
        lab_sem=dma((2, 2 * s.x)),
        laby_sem=dma((2, s.y)),
        cnt_sem=dma((2, s.x)),
        cnty_sem=dma((2, s.y)),
        stx_sem=dma((3, 2, 2 * s.x)),
        sty_sem=dma((3, 2, s.y)),
        mw_sem=dma((2, 2, s.z)),
        num_sem=dma((2, 2, 3 * s.z)),
        new_sem=dma((2, 2 * s.z)),
        out_sem=dma((2, s.z)),
    )


def kernel(s, names, emb, lab, qr, pos, out_c, out_v, *scratch):
    ref = dict(zip(names, scratch))
    dp, cent = lax.axis_index("dp"), lax.axis_index("cent")
    z, core = dp // 2, dp % 2
    y, x = cent // s.x, cent % s.x

    def device(z_, core_, y_, x_):
        return (z_ * 2 + core_, y_ * s.x + x_)

    to_z = lambda p: device(p, core, y, x)
    to_y = lambda p: device(z, core, p, x)
    to_x = lambda p: device(z, core, y, p)
    to_cx = lambda p: device(z, p // s.x, y, p % s.x)
    partner = device(z, 1 - core, y, x)
    cx = core * s.x + x

    def each(n, me, do):
        def step(i, carry):
            do(lax.rem(me + i, n))
            return carry

        lax.fori_loop(1, n, step, 0)

    def copy(src, dst, sems, out_index, in_index, to):
        return pltpu.make_async_remote_copy(
            src_ref=src,
            dst_ref=dst,
            send_sem=sems.at[0, out_index],
            recv_sem=sems.at[1, in_index],
            device_id=to,
            device_id_type=MESH,
        )

    pending = []

    class Exchange:
        def __init__(self, n, me, to, sems, src, dst):
            self.n, self.me, self.to, self.sems, self.src, self.dst = n, me, to, sems, src, dst

        def start(self):
            each(self.n, self.me, lambda p: copy(
                self.src(p), self.dst(self.me), self.sems, p, self.me, self.to(p)).start())
            pending.append(self)

        def arrived(self):
            each(self.n, self.me, lambda p: copy(
                self.src(p), self.dst(p), self.sems, p, p, self.to(p)).wait_recv())

        def sent(self):
            each(self.n, self.me, lambda p: copy(
                self.src(p), self.dst(self.me), self.sems, p, self.me, self.to(p)).wait_send())

    barrier = pltpu.get_barrier_semaphore()

    def greet(to):
        return lambda p: pl.semaphore_signal(barrier, inc=1, device_id=to(p), device_id_type=MESH)

    each(2 * s.x, cx, greet(to_cx))
    each(s.y, y, greet(to_y))
    each(s.z, z, greet(to_z))
    pl.semaphore_wait(barrier, 2 * s.x - 1 + s.y - 1 + s.z - 1)

    mine, theirs = ref["mine"], ref["theirs"]
    mine[...] = jnp.concatenate(
        [emb[...].astype(F32), jnp.zeros((32 - s.rows, s.features), F32)], axis=0
    ).astype(BF16)
    swap = pltpu.make_async_remote_copy(
        src_ref=mine, dst_ref=theirs, send_sem=ref["core_sem"].at[0],
        recv_sem=ref["core_sem"].at[1], device_id=partner, device_id_type=MESH,
    )
    swap.start()

    lab_x = ref["lab_x"]
    lab_x[core, x] = lab[...]
    swap.wait_recv()
    rows, block = ref["rows"], ref["block"]
    own = mine[...].astype(F32)[: s.rows]
    other = theirs[...].astype(F32)[: s.rows]
    first = jnp.where(core == 0, own, other)
    second = jnp.where(core == 0, other, own)
    block[...] = jnp.concatenate([first, second], axis=0).astype(BF16)

    def near_first(j):
        far = (j + 1) // 2
        return lax.rem(y + jnp.where(j % 2 == 1, far, s.y - far), s.y)

    class Plane:
        def __init__(self, t, at, row, use):
            self.at, self.row, self.use = at, row, use
            self.sems = {name: ref[name + "_sem"].at[t] for name in ("share", "a1", "a2", "b1", "b2")}

        def a1(self, p, source):
            piece = self.at(y, source, 0)
            return copy(piece, piece, self.sems["a1"], p, source, to_x(p))

        def a2(self, p, source):
            piece = self.at(source, everything, 0)
            return copy(piece, piece, self.sems["a2"], p, source, to_y(p))

        def b1(self, k, p, source):
            piece = self.at(source, x, k)
            first = (k - 1) * s.y
            return copy(piece, piece, self.sems["b1"], first + p, first + source, to_y(p))

        def b2(self, k, yy, p, source):
            piece = self.at(yy, source, k)
            first = ((k - 1) * s.y + yy) * s.x
            return copy(piece, piece, self.sems["b2"], first + p, first + source, to_x(p))

        def share(self, yy, side):
            piece = self.row(yy, side)
            return copy(piece, piece, self.sems["share"], yy, yy, partner)

        def along_y(self, do):
            def step(j, carry):
                do(near_first(j))
                return carry

            lax.fori_loop(1, s.y, step, 0)

        def start_a(self):
            each(s.x, x, lambda p: self.a1(p, x).start())

        def start_b(self, k):
            self.along_y(lambda p: self.b1(k, p, y).start())
            each(s.x, x, lambda p: self.b2(k, y, p, x).start())

        def sent(self):
            each(s.x, x, lambda p: self.a1(p, x).wait_send())
            self.along_y(lambda p: self.a2(p, y).wait_send())
            for k in (1, 2):
                self.along_y(lambda p: self.b1(k, p, y).wait_send())

            def step(yy, carry):
                for k in (1, 2):
                    each(s.x, x, lambda p: self.b2(k, yy, p, x).wait_send())
                self.share(yy, core).wait_send()
                return carry

            lax.fori_loop(0, s.y, step, 0)

        def spread(self, k, low, high):
            def step(j, carry):
                source = near_first(j)
                self.b1(k, source, source).wait_recv()
                each(s.x, x, lambda p: self.b2(k, source, p, x).start())
                return carry

            lax.fori_loop(low, high, step, 0)

        def turn(self):
            each(s.x, x, lambda p: self.a1(p, p).wait_recv())
            self.along_y(lambda p: self.a2(p, y).start())

        def finish(self):
            def step(j, carry):
                @pl.when(j < s.y)
                def _():
                    source = near_first(j)

                    @pl.when(j > 0)
                    def _():
                        self.a2(source, source).wait_recv()

                    for k in (1, 2):
                        each(s.x, x, lambda p: self.b2(k, source, p, p).wait_recv())
                    self.share(source, core).start()

                @pl.when(j > 0)
                def _():
                    source = near_first(j - 1)
                    self.share(source, 1 - core).wait_recv()
                    self.use(source)

                return carry

            lax.fori_loop(0, s.y + 1, step, 0)

    def lanes_of(c):
        return pl.ds(pl.multiple_of(c * s.half, 128), s.half)

    logits, probs = ref["logits"], ref["probs"]
    cents = ref["cents"]
    everything = slice(None)

    def rows_of(b, lanes):
        return rows[b, :, :, lanes].reshape(s.width, -1)

    def products_of(t):
        def use(b):
            logits[b] = lax.dot_general(
                cents[t], rows_of(b, everything), (((1,), (1,)), ((), ())), preferred_element_type=F32
            )

        return use

    rows[y, x, :, lanes_of(core)] = block[:, lanes_of(core)]
    quarter = s.half // 4
    row_parts = ((0, quarter), (quarter, s.half - 2 * quarter), (s.half - quarter, quarter))

    def rows_at(yy, xx, k):
        start, size = row_parts[k]
        return rows.at[yy, xx, :, pl.ds(pl.multiple_of(core * s.half + start, 128), size)]

    gather = Plane(0, rows_at, lambda yy, c: rows.at[yy, :, :, lanes_of(c)], products_of(0))
    pending.append(gather)
    gather.start_a()
    gather.start_b(1)
    gather.start_b(2)

    zh = s.z // 2

    def cent_copy(src_z, to):
        place = pl.ds(pl.multiple_of((src_z % zh) * s.chip, 16), s.chip)
        return copy(block, cents.at[0, place, :], ref["cent_sem"], to, src_z, to_z(to))

    @pl.when(z // zh == core)
    def _():
        each(s.z, z, lambda p: cent_copy(z, p).start())
        cents[0, pl.ds(pl.multiple_of((z % zh) * s.chip, 16), s.chip), :] = block[...]

    lab_ex = Exchange(2 * s.x, cx, to_cx, ref["lab_sem"],
                      lambda p: lab_x.at[core, x], lambda p: lab_x.at[p // s.x, p % s.x])
    lab_ex.start()

    cnt_s, cnt_x = ref["cnt_s"], ref["cnt_x"]
    places = lax.broadcasted_iota(jnp.int32, (s.lanes, s.seeds), 0)
    hot_r = jnp.where(places == qr[1:2, :], 1.0, 0.0).astype(BF16)
    for xx in range(s.x):
        owner = lax.broadcasted_iota(jnp.int32, (s.y, s.seeds), 0) * s.x + (xx + core * s.x * s.y)
        hot_q = jnp.where(owner == qr[0:1, :], 1.0, 0.0).astype(BF16)
        cnt_s[xx] = lax.dot_general(hot_q, hot_r, (((1,), (1,)), ((), ())), preferred_element_type=F32)
    cnt_ex = Exchange(s.x, x, to_x, ref["cnt_sem"], lambda p: cnt_s.at[p], lambda p: cnt_x.at[p])
    cnt_ex.start()
    gather.spread(1, 1, s.y)
    gather.turn()

    cnt_ex.arrived()
    cnt_x[x] = cnt_s[x]
    total = cnt_x[0]
    for xx in range(1, s.x):
        total = total + cnt_x[xx]
    cnt_t, cnt_y = ref["cnt_t"], ref["cnt_y"]
    for yy in range(s.y):
        cnt_t[yy] = total[yy : yy + 1]
    cnty_ex = Exchange(s.y, y, to_y, ref["cnty_sem"], lambda p: cnt_t.at[p], lambda p: cnt_y.at[p])
    cnty_ex.start()
    lab_ex.arrived()
    lab_y = ref["lab_y"]
    line = lab_x[0, 0]
    for i in range(1, 2 * s.x):
        line = line + lab_x[i // s.x, i % s.x]
    lab_y[y] = line
    laby_ex = Exchange(s.y, y, to_y, ref["laby_sem"], lambda p: lab_y.at[y], lambda p: lab_y.at[p])
    laby_ex.start()

    def cents_in(i, carry):
        src_z = core * zh + i

        @pl.when(src_z != z)
        def _():
            place = pl.ds(pl.multiple_of(i * s.chip, 16), s.chip)
            copy(block, cents.at[0, place, :], ref["cent_sem"], src_z, src_z, to_z(src_z)).wait_recv()

        return carry

    gather.spread(2, 1, s.y)
    lax.fori_loop(0, zh, cents_in, 0)
    gather.finish()

    def to_column(row):
        eye = lax.broadcasted_iota(jnp.int32, (s.local, s.lanes), 0) == lax.broadcasted_iota(
            jnp.int32, (s.local, s.lanes), 1
        )
        return jnp.sum(jnp.where(eye, row, 0.0), axis=1, keepdims=True)

    cnty_ex.arrived()
    cnt_y[y] = cnt_t[y]
    line = cnt_y[0]
    for yy in range(1, s.y):
        line = line + cnt_y[yy]
    weight = to_column(line)
    laby_ex.arrived()

    @pl.when(z // zh == core)
    def _():
        each(s.z, z, lambda p: cent_copy(z, p).wait_send())

    ref["st_s"][...] = jnp.zeros_like(ref["st_s"])

    def blocks(do):
        def step(b, carry):
            do(2 * b)
            do(2 * b + 1)
            return carry

        lax.fori_loop(0, s.y // 2, step, 0)

    def lse_of(parts):
        top = functools.reduce(jnp.maximum, parts)
        return top + jnp.log(sum(jnp.exp(part - top) for part in parts))

    def total_of(parts):
        return sum(parts)

    def all_reduce(t, combine):
        st_s, st_x, st_t, st_y = (ref[name].at[t] for name in ("st_s", "st_x", "st_t", "st_y"))
        near = Exchange(2 * s.x, cx, to_cx, ref["stx_sem"].at[t], lambda p: st_s, lambda p: st_x.at[p // s.x, p % s.x])
        far = Exchange(s.y, y, to_y, ref["sty_sem"].at[t], lambda p: st_t, lambda p: st_y.at[p])
        near.start()
        yield
        near.arrived()
        st_x[core, x] = st_s[...]
        st_t[...] = combine([st_x[i // s.x, i % s.x] for i in range(2 * s.x)])
        far.start()
        yield
        far.arrived()
        st_y[y] = st_t[...]
        ref["st_f"][t] = combine([st_y[i] for i in range(s.y)])

    table, wide = ref["table"], ref["wide"]

    def widen(yy):
        size = s.x * s.local
        for a in range(2):
            wide[pl.ds(pl.multiple_of((a * s.y + yy) * size, 16), size), :] = (
                table[a, yy].reshape(size, s.slab).astype(F32)
            )

    low = max(16, s.local // 6 // 16 * 16)
    rest = (s.local - low) // 32 * 16
    new_parts = ((0, rest), (rest, s.local - low - rest), (s.local - low, low))

    def table_at(yy, xx, k):
        start, size = new_parts[(k + 2) % 3]
        return table.at[core, yy, xx, pl.ds(start, size), :]

    gather = Plane(1, table_at, lambda yy, c: table.at[c, yy], widen)
    pending.append(gather)

    for t in range(2):
        held = cents.at[t]
        exact = held[...].astype(F32)
        norm = jnp.sum(exact * exact, axis=1, keepdims=True)
        bias = jnp.where(weight > 0.0, (-0.5 * INVERSE_TEMP) * norm, ABSENT)
        st_s = ref["st_s"].at[t]

        if t == 1:
            blocks(products_of(1))

        def scores_of(b):
            value = jnp.where(weight > 0.0, INVERSE_TEMP * logits[b] + bias, ABSENT)
            logits[b] = value
            top = jnp.max(value, axis=0, keepdims=True)
            mass = jnp.sum(weight * jnp.exp(value - top), axis=0, keepdims=True)
            st_s[b, :, : s.width] = jnp.maximum(top + jnp.log(mass), ABSENT)

        blocks(scores_of)
        for _ in all_reduce(t, lse_of):
            pass
        norm_of = ref["st_f"].at[t]
        mw_s, mw_r = ref["mw_s"].at[t], ref["mw_r"].at[t]
        mw_s[...] = jnp.zeros_like(mw_s)

        def shares_of(b):
            value = jnp.exp(logits[b] - norm_of[b, :, : s.width])
            if t == 1:
                logits[b] = value
            rounded = value.astype(BF16)
            probs[b] = rounded
            label = lab_y[b, :, : s.width]
            line = lax.broadcasted_iota(jnp.int32, (8, s.width), 0)
            left = jnp.where(line == 0, 1.0, jnp.where(line == 1, label, 0.0)).astype(BF16)
            both = lax.dot_general(left, rounded, (((1,), (1,)), ((), ())), preferred_element_type=F32)
            mw_s[:, : s.local] += both

        blocks(shares_of)
        mw_ex = Exchange(s.z, z, to_z, ref["mw_sem"].at[t], lambda p: mw_s, lambda p: mw_r.at[p])
        mw_ex.start()

        num_s, num_r = ref["num_s"].at[t], ref["num_r"].at[t]
        half = s.local // 2
        parts = ((0, half), (half, half)) if t == 0 else new_parts

        def num_copy(k, p, source):
            piece = pl.ds(parts[k][0], parts[k][1])
            return copy(num_s.at[p, piece, :], num_r.at[source, piece, :], ref["num_sem"].at[t],
                        k * s.z + p, k * s.z + source, to_z(p))

        pairs = s.z // 2

        def numer_of(i, carry):
            pair = lax.rem(z // 2 + 1 + i, pairs)
            lanes = pl.ds(pl.multiple_of(pair * 2 * s.slab, 128), 2 * s.slab)
            acc = jnp.zeros((s.local, 2 * s.slab), F32)
            for b in range(s.y):
                acc = acc + jnp.dot(probs[b], rows_of(b, lanes), preferred_element_type=F32)
            for side in range(2):
                p = pair * 2 + side
                num_s[p] = acc[:, side * s.slab : (side + 1) * s.slab].astype(BF16)

                @pl.when(p != z)
                def _():
                    num_copy(0, p, z).start()

            return carry

        lax.fori_loop(0, pairs, numer_of, 0)
        for k in range(1, len(parts)):
            each(s.z, z, lambda p: num_copy(k, p, z).start())
        mw_ex.arrived()
        mw_r[z] = mw_s[...]
        both = mw_r[0]
        for i in range(1, s.z):
            both = both + mw_r[i]
        mass = to_column(both[0:1])
        if t == 1:
            wins = to_column(both[1:2])
            rate = weight * ((wins + 0.5 * PSEUDO_COUNT) / (mass + PSEUDO_COUNT))
            sc = ref["st_s"].at[2]

            def step_scores(b):
                sc[b, :, : s.width] = jnp.sum(logits[b] * rate, axis=0, keepdims=True)

            blocks(step_scores)
            reduce_scores = all_reduce(2, total_of)
            next(reduce_scores)
        mylanes = pl.ds(pl.multiple_of(z * s.slab, 128), s.slab)

        def fresh(k):
            each(s.z, z, lambda p: num_copy(k, p, p).wait_recv())
            first, size = parts[k]
            piece = slice(first, first + size)
            num_r[z, piece, :] = num_s[z, piece, :]
            acc = num_r[0, piece, :].astype(F32)
            for i in range(1, s.z):
                acc = acc + num_r[i, piece, :].astype(F32)
            acc = acc + PSEUDO_COUNT * held[piece, mylanes].astype(F32)
            return (acc / (mass[piece] + PSEUDO_COUNT)).astype(BF16)

        if t == 0:
            def new_copy(k, p, source):
                lanes = pl.ds(pl.multiple_of(source * s.slab, 128), s.slab)
                piece = cents.at[1, pl.ds(parts[k][0], parts[k][1]), lanes]
                return copy(piece, piece, ref["new_sem"], k * s.z + p, k * s.z + source, to_z(p))

            for k in range(2):
                cents[1, parts[k][0] : parts[k][0] + parts[k][1], mylanes] = fresh(k)
                each(s.z, z, lambda p: new_copy(k, p, z).start())
            for k in range(2):
                each(s.z, z, lambda p: new_copy(k, p, p).wait_recv())
        else:
            for k in range(3):
                table[core, y, x, parts[k][0] : parts[k][0] + parts[k][1], :] = fresh(k)
                if k < 2:
                    gather.start_b(k + 1)
                else:
                    gather.start_a()
            for k in range(3):
                each(s.z, z, lambda p: num_copy(k, p, z).wait_send())
        if t == 0:
            for k in range(2):
                each(s.z, z, lambda p: num_copy(k, p, z).wait_send())
                each(s.z, z, lambda p: new_copy(k, p, z).wait_send())

    next(reduce_scores)
    gather.spread(1, 1, s.y)
    gather.turn()
    gather.spread(2, 1, s.y)
    for _ in reduce_scores:
        pass
    gather.finish()
    final = ref["st_f"]
    offset = x * s.chip + core * s.rows
    n_out = 32
    here = lax.broadcasted_iota(jnp.int32, (n_out, s.span), 1)
    wanted = lax.broadcasted_iota(jnp.int32, (n_out, s.span), 0) + offset
    column = jnp.sum(jnp.where(here == wanted, final[2, y], 0.0), axis=1, keepdims=True)
    eye = lax.broadcasted_iota(jnp.int32, (n_out, 128), 0) == lax.broadcasted_iota(jnp.int32, (n_out, 128), 1)
    out_v[...] = jnp.sum(jnp.where(eye, column, 0.0), axis=0, keepdims=True)

    picked, out_s, out_r = ref["picked"], ref["out_s"], ref["out_r"]
    out_ex = Exchange(s.z, z, to_z, ref["out_sem"], lambda p: out_s.at[p], lambda p: out_r.at[p])

    def pick(i, carry):
        p = lax.rem(z + 1 + i, s.z)
        base = (2 * p + core) * s.outs

        def eight(j, carry):
            for k in range(8):
                n = j * 8 + k
                picked[pl.ds(n, 1), :] = wide[pl.ds(pos[base + n], 1), :]
            return carry

        lax.fori_loop(0, s.outs // 8, eight, 0)
        out_s[p] = picked[...].astype(BF16)

        @pl.when(p != z)
        def _():
            copy(out_s.at[p], out_r.at[z], ref["out_sem"], p, z, to_z(p)).start()

        return carry

    lax.fori_loop(0, s.z, pick, 0)
    pending.append(out_ex)
    out_ex.arrived()
    out_r[z] = out_s[z]
    for i in range(s.z):
        out_c[:, i * s.slab : (i + 1) * s.slab] = out_r[i]
    swap.wait_send()
    for exchange in pending:
        exchange.sent()


def per_device(s, embeddings, outcomes, seed_index):
    core = lax.axis_index("dp") % 2
    cent = lax.axis_index("cent")
    plane = s.rows * s.x * s.y
    dp, rest = seed_index // plane, seed_index % plane
    zs, side = dp // 2, dp % 2
    zh = s.z // 2
    q = (zs // zh) * (s.x * s.y) + rest // s.rows
    r = (zs % zh) * s.chip + side * s.rows + rest % s.rows
    qr = jnp.stack([q, r])
    pos = q * s.local + r
    offset = (cent % s.x) * s.chip + core * s.rows
    spot = lax.broadcasted_iota(jnp.int32, (s.rows, s.span), 1) - lax.broadcasted_iota(
        jnp.int32, (s.rows, s.span), 0
    )
    lab = jnp.sum(
        jnp.where(spot == offset, outcomes.astype(F32)[:, None], 0.0), axis=0, keepdims=True
    )
    scratch = scratch_of(s)
    vmem = pl.BlockSpec(memory_space=pltpu.VMEM)
    out_c, out_v = pl.pallas_call(
        functools.partial(kernel, s, tuple(scratch)),
        out_shape=(
            jax.ShapeDtypeStruct((s.outs, s.features), BF16),
            jax.ShapeDtypeStruct((1, 128), F32),
        ),
        in_specs=[vmem, vmem, vmem, pl.BlockSpec(memory_space=pltpu.SMEM)],
        out_specs=(vmem, vmem),
        scratch_shapes=list(scratch.values()),
        compiler_params=pltpu.CompilerParams(
            collective_id=0, has_side_effects=True, vmem_limit_bytes=48 * 1024 * 1024
        ),
    )(embeddings, lab, qr, pos)
    return out_c, out_v[0, : s.rows]


def build(mesh, y, x):
    z = mesh.shape["dp"] // 2

    def run(embeddings, outcomes, seed_index):
        devices = mesh.shape["dp"] * mesh.shape["cent"]
        s = Sizes(
            z, y, x, embeddings.shape[0] // devices, embeddings.shape[1],
            seed_index.shape[0] // mesh.shape["cent"],
        )
        return jax.shard_map(
            functools.partial(per_device, s),
            mesh=mesh,
            in_specs=(P(("dp", "cent"), None), P(("dp", "cent")), P("cent")),
            out_specs=(P(("cent", "dp"), None), P(("dp", "cent"))),
            check_vma=False,
        )(embeddings, outcomes, seed_index)

    return run


def solution(mesh):
    return build(mesh, mesh.shape["cent"] // 4, 4)
```

time: 138 us -> 130 us (0.942)
  Pallas kernels: 135 us -> 127 us
    pallas_call x1, Pallas kernels: 135 us -> 127 us  [per_device(): pl.pallas_call(functools.partial(kernel, s, tuple(scratch)), out_shape=(j...]
where the time goes in v2:
time: 130 us
  Pallas kernels  127 us (98%)
  local copies, waits for them, and re-layouts  1.79 us (1%)
    pallas_call x1, Pallas kernels, per_device(): pl.pallas_call(functools.partial(kernel, s, tuple(scratch)), out_shape=(j...  127 us

profile of v2, /device:TPU:1, one launch (start us, length us, event | category | flops | bytes accessed | tf_op | source)
XLA Modules:
  0.0 129.8 jit_solution(4753730294112165153)
XLA Ops:
  0.6 0.0 copy-start.2
  0.6 0.0 copy-start
  0.7 0.0 copy-start.1
  0.7 0.6 copy-done.2
  1.3 0.1 select_reduce_fusion
  1.4 0.0 copy-done.1
  1.4 0.0 copy-done
  1.5 127.2 %shard_map.50 = (bf16[64,1024]{1,0:T(8,128)(2,1)S(1)}, f32[1,128]{1,0:T(1,128)S(1)}) custom-call(bf16[24,1024]{1,0:T(8,128)(2,1)S(1)} %copy-done, f32[1,256]{1,0:T(1,128)S(1)} %bitcast.5, s32[2,1024]{1,0:T(2,128)S(1)} %pad_add_fusion.qr, s32[1024]{0:T(1024)S(1)} %get-tuple-element.6.pos), custom_call_target="tpu_custom_call" | custom-call | tf_op jit(solution)/shard_map/pallas_call | solution.py:620
  128.6 0.5 slice_bitcast_fusion
  129.1 0.7 copy.6
  (3 shorter events, 0.0 us)
Async XLA Ops:
  0.6 0.7 copy-start.2
  0.6 0.8 copy-start
  0.7 0.7 copy-start.1

commit v3 on v2

--- a/solution.py
+++ b/solution.py
@@ -36,6 +36,11 @@
     dma = pltpu.SemaphoreType.DMA
     v = pltpu.VMEM
     return dict(
+        qr=v((2, s.seeds), jnp.int32),
+        pos=pltpu.SMEM((s.seeds,), jnp.int32),
+        score=v((1, 128), F32),
+        in_sem=dma((4,)),
+        store_sem=dma((s.z + 1,)),
         mine=v((32, s.features), BF16),
         theirs=v((32, s.features), BF16),
         block=v((s.chip, s.features), BF16),
@@ -48,6 +53,7 @@
         cnt_t=v((s.y, 1, s.lanes), F32),
         cnt_y=v((s.y, 1, s.lanes), F32),
         logits=v((s.y, s.local, s.width), F32),
+        tops=v((s.y, 1, s.width), F32),
         probs=v((s.y, s.local, s.width), BF16),
         st_s=v((3, s.y, 1, s.span), F32),
         st_x=v((3, 2, s.x, s.y, 1, s.span), F32),
@@ -83,8 +89,9 @@
     )
 
 
-def kernel(s, names, emb, lab, qr, pos, out_c, out_v, *scratch):
+def kernel(s, names, emb, lab, qr_in, pos_in, out_c, out_v, *scratch):
     ref = dict(zip(names, scratch))
+    mine, theirs, qr, pos, lab_x = (ref[name] for name in ("mine", "theirs", "qr", "pos", "lab_x"))
     dp, cent = lax.axis_index("dp"), lax.axis_index("cent")
     z, core = dp // 2, dp % 2
     y, x = cent // s.x, cent % s.x
@@ -135,6 +142,12 @@
             each(self.n, self.me, lambda p: copy(
                 self.src(p), self.dst(self.me), self.sems, p, self.me, self.to(p)).wait_send())
 
+    loads = [
+        pltpu.make_async_copy(src, dst, ref["in_sem"].at[i])
+        for i, (src, dst) in enumerate(((emb, mine), (lab, lab_x.at[core, x]), (qr_in, qr), (pos_in, pos)))
+    ]
+    for load in loads:
+        load.start()
     barrier = pltpu.get_barrier_semaphore()
 
     def greet(to):
@@ -145,18 +158,13 @@
     each(s.z, z, greet(to_z))
     pl.semaphore_wait(barrier, 2 * s.x - 1 + s.y - 1 + s.z - 1)
 
-    mine, theirs = ref["mine"], ref["theirs"]
-    mine[...] = jnp.concatenate(
-        [emb[...].astype(F32), jnp.zeros((32 - s.rows, s.features), F32)], axis=0
-    ).astype(BF16)
+    loads[0].wait()
     swap = pltpu.make_async_remote_copy(
         src_ref=mine, dst_ref=theirs, send_sem=ref["core_sem"].at[0],
         recv_sem=ref["core_sem"].at[1], device_id=partner, device_id_type=MESH,
     )
     swap.start()
 
-    lab_x = ref["lab_x"]
-    lab_x[core, x] = lab[...]
     swap.wait_recv()
     rows, block = ref["rows"], ref["block"]
     own = mine[...].astype(F32)[: s.rows]
@@ -264,7 +272,7 @@
     def lanes_of(c):
         return pl.ds(pl.multiple_of(c * s.half, 128), s.half)
 
-    logits, probs = ref["logits"], ref["probs"]
+    logits, probs, tops = ref["logits"], ref["probs"], ref["tops"]
     cents = ref["cents"]
     everything = slice(None)
 
@@ -306,7 +314,10 @@
 
     lab_ex = Exchange(2 * s.x, cx, to_cx, ref["lab_sem"],
                       lambda p: lab_x.at[core, x], lambda p: lab_x.at[p // s.x, p % s.x])
+    loads[1].wait()
     lab_ex.start()
+    loads[2].wait()
+    loads[3].wait()
 
     cnt_s, cnt_x = ref["cnt_s"], ref["cnt_x"]
     places = lax.broadcasted_iota(jnp.int32, (s.lanes, s.seeds), 0)
@@ -412,7 +423,7 @@
                 table[a, yy].reshape(size, s.slab).astype(F32)
             )
 
-    low = max(16, s.local // 6 // 16 * 16)
+    low = 48
     rest = (s.local - low) // 32 * 16
     new_parts = ((0, rest), (rest, s.local - low - rest), (s.local - low, low))
 
@@ -435,9 +446,11 @@
 
         def scores_of(b):
             value = jnp.where(weight > 0.0, INVERSE_TEMP * logits[b] + bias, ABSENT)
-            logits[b] = value
             top = jnp.max(value, axis=0, keepdims=True)
-            mass = jnp.sum(weight * jnp.exp(value - top), axis=0, keepdims=True)
+            power = jnp.exp(value - top)
+            logits[b] = power
+            tops[b] = top
+            mass = jnp.sum(weight * power, axis=0, keepdims=True)
             st_s[b, :, : s.width] = jnp.maximum(top + jnp.log(mass), ABSENT)
 
         blocks(scores_of)
@@ -448,7 +461,7 @@
         mw_s[...] = jnp.zeros_like(mw_s)
 
         def shares_of(b):
-            value = jnp.exp(logits[b] - norm_of[b, :, : s.width])
+            value = logits[b] * jnp.exp(tops[b] - norm_of[b, :, : s.width])
             if t == 1:
                 logits[b] = value
             rounded = value.astype(BF16)
@@ -554,7 +567,6 @@
     gather.spread(2, 1, s.y)
     for _ in reduce_scores:
         pass
-    gather.finish()
     final = ref["st_f"]
     offset = x * s.chip + core * s.rows
     n_out = 32
@@ -562,8 +574,10 @@
     wanted = lax.broadcasted_iota(jnp.int32, (n_out, s.span), 0) + offset
     column = jnp.sum(jnp.where(here == wanted, final[2, y], 0.0), axis=1, keepdims=True)
     eye = lax.broadcasted_iota(jnp.int32, (n_out, 128), 0) == lax.broadcasted_iota(jnp.int32, (n_out, 128), 1)
-    out_v[...] = jnp.sum(jnp.where(eye, column, 0.0), axis=0, keepdims=True)
-
+    ref["score"][...] = jnp.sum(jnp.where(eye, column, 0.0), axis=0, keepdims=True)
+    store_score = pltpu.make_async_copy(ref["score"], out_v, ref["store_sem"].at[s.z])
+    store_score.start()
+    gather.finish()
     picked, out_s, out_r = ref["picked"], ref["out_s"], ref["out_r"]
     out_ex = Exchange(s.z, z, to_z, ref["out_sem"], lambda p: out_s.at[p], lambda p: out_r.at[p])
 
@@ -588,13 +602,25 @@
 
     lax.fori_loop(0, s.z, pick, 0)
     pending.append(out_ex)
-    out_ex.arrived()
-    out_r[z] = out_s[z]
-    for i in range(s.z):
-        out_c[:, i * s.slab : (i + 1) * s.slab] = out_r[i]
+    def store(p, block):
+        lanes = pl.ds(pl.multiple_of(p * s.slab, 128), s.slab)
+        return pltpu.make_async_copy(block, out_c.at[:, lanes], ref["store_sem"].at[p])
+
+    store(z, out_s.at[z]).start()
+
+    def keep(i, carry):
+        p = lax.rem(z + s.z - i, s.z)
+        copy(out_s.at[p], out_r.at[p], ref["out_sem"], p, p, to_z(p)).wait_recv()
+        store(p, out_r.at[p]).start()
+        return carry
+
+    lax.fori_loop(1, s.z, keep, 0)
     swap.wait_send()
     for exchange in pending:
         exchange.sent()
+    store_score.wait()
+    store(z, out_s.at[z]).wait()
+    each(s.z, z, lambda p: store(p, out_r.at[p]).wait())
 
 
 def per_device(s, embeddings, outcomes, seed_index):
@@ -616,20 +642,21 @@
         jnp.where(spot == offset, outcomes.astype(F32)[:, None], 0.0), axis=0, keepdims=True
     )
     scratch = scratch_of(s)
-    vmem = pl.BlockSpec(memory_space=pltpu.VMEM)
+    anywhere = pl.BlockSpec(memory_space=pl.ANY)
+    padded = jnp.pad(embeddings, ((0, 32 - s.rows), (0, 0)))
     out_c, out_v = pl.pallas_call(
         functools.partial(kernel, s, tuple(scratch)),
         out_shape=(
             jax.ShapeDtypeStruct((s.outs, s.features), BF16),
             jax.ShapeDtypeStruct((1, 128), F32),
         ),
-        in_specs=[vmem, vmem, vmem, pl.BlockSpec(memory_space=pltpu.SMEM)],
-        out_specs=(vmem, vmem),
+        in_specs=[anywhere] * 4,
+        out_specs=(anywhere, anywhere),
         scratch_shapes=list(scratch.values()),
         compiler_params=pltpu.CompilerParams(
             collective_id=0, has_side_effects=True, vmem_limit_bytes=48 * 1024 * 1024
         ),
-    )(embeddings, lab, qr, pos)
+    )(padded, lab, qr, pos)
     return out_c, out_v[0, : s.rows]
 
 

time: 130 us -> 129 us (level)
  no operation moved by 1% of the time
where the time goes in v3:
time: 129 us
  Pallas kernels  127 us (98%)
  local copies, waits for them, and re-layouts  1.8 us (1%)
    pallas_call x1, Pallas kernels, per_device(): pl.pallas_call(functools.partial(kernel, s, tuple(scratch)), out_shape=(j...  127 us

profile of v3, /device:TPU:1, one launch (start us, length us, event | category | flops | bytes accessed | tf_op | source)
XLA Modules:
  0.0 129.3 jit_solution(2635179583901238969)
XLA Ops:
  0.6 0.0 copy-start.2
  0.6 0.0 copy-start
  0.7 0.0 copy-start.1
  0.7 0.6 copy-done.2
  1.3 0.1 select_reduce_fusion
  1.4 0.0 copy-done.1
  1.4 0.0 copy-done
  1.5 126.6 %shard_map.50 = (bf16[64,1024]{1,0:T(8,128)(2,1)S(1)}, f32[1,128]{1,0:T(1,128)S(1)}) custom-call(bf16[32,1024]{1,0:T(8,128)(2,1)S(1)} %pad.4.emb, f32[1,256]{1,0:T(1,128)S(1)} %bitcast.5, s32[2,1024]{1,0:T(2,128)S(1)} %pad_add_fusion.qr_in, s32[1024]{0:T(1024)S(1)} %get-tuple-element.6.pos_in), custom_call_target="tpu_custom_call" | custom-call | tf_op jit(solution)/shard_map/pallas_call | solution.py:647
  128.1 0.5 slice_bitcast_fusion
  128.6 0.7 copy.6
  (4 shorter events, 0.1 us)
Async XLA Ops:
  0.6 0.7 copy-start.2
  0.6 0.8 copy-start
  0.7 0.7 copy-start.1

commit v4 on v3

--- a/solution.py
+++ b/solution.py
@@ -124,6 +124,7 @@
         )
 
     pending = []
+    later = []
 
     class Exchange:
         def __init__(self, n, me, to, sems, src, dst):
@@ -378,10 +379,6 @@
     weight = to_column(line)
     laby_ex.arrived()
 
-    @pl.when(z // zh == core)
-    def _():
-        each(s.z, z, lambda p: cent_copy(z, p).wait_send())
-
     ref["st_s"][...] = jnp.zeros_like(ref["st_s"])
 
     def blocks(do):
@@ -480,7 +477,7 @@
         half = s.local // 2
         parts = ((0, half), (half, half)) if t == 0 else new_parts
 
-        def num_copy(k, p, source):
+        def num_copy(k, p, source, t=t, parts=parts, num_s=num_s, num_r=num_r):
             piece = pl.ds(parts[k][0], parts[k][1])
             return copy(num_s.at[p, piece, :], num_r.at[source, piece, :], ref["num_sem"].at[t],
                         k * s.z + p, k * s.z + source, to_z(p))
@@ -537,7 +534,7 @@
             return (acc / (mass[piece] + PSEUDO_COUNT)).astype(BF16)
 
         if t == 0:
-            def new_copy(k, p, source):
+            def new_copy(k, p, source, parts=parts):
                 lanes = pl.ds(pl.multiple_of(source * s.slab, 128), s.slab)
                 piece = cents.at[1, pl.ds(parts[k][0], parts[k][1]), lanes]
                 return copy(piece, piece, ref["new_sem"], k * s.z + p, k * s.z + source, to_z(p))
@@ -554,12 +551,9 @@
                     gather.start_b(k + 1)
                 else:
                     gather.start_a()
-            for k in range(3):
-                each(s.z, z, lambda p: num_copy(k, p, z).wait_send())
+        later.append((num_copy, len(parts)))
         if t == 0:
-            for k in range(2):
-                each(s.z, z, lambda p: num_copy(k, p, z).wait_send())
-                each(s.z, z, lambda p: new_copy(k, p, z).wait_send())
+            later.append((new_copy, 2))
 
     next(reduce_scores)
     gather.spread(1, 1, s.y)
@@ -601,7 +595,17 @@
         return carry
 
     lax.fori_loop(0, s.z, pick, 0)
-    pending.append(out_ex)
+    swap.wait_send()
+
+    @pl.when(z // zh == core)
+    def _():
+        each(s.z, z, lambda p: cent_copy(z, p).wait_send())
+
+    for exchange in pending:
+        exchange.sent()
+    for sent_copy, count in later:
+        for k in range(count):
+            each(s.z, z, lambda p: sent_copy(k, p, z).wait_send())
     def store(p, block):
         lanes = pl.ds(pl.multiple_of(p * s.slab, 128), s.slab)
         return pltpu.make_async_copy(block, out_c.at[:, lanes], ref["store_sem"].at[p])
@@ -615,9 +619,7 @@
         return carry
 
     lax.fori_loop(1, s.z, keep, 0)
-    swap.wait_send()
-    for exchange in pending:
-        exchange.sent()
+    out_ex.sent()
     store_score.wait()
     store(z, out_s.at[z]).wait()
     each(s.z, z, lambda p: store(p, out_r.at[p]).wait())

time: 129 us -> 125 us (0.969)
  Pallas kernels: 127 us -> 122 us
    pallas_call x1, Pallas kernels: 127 us -> 122 us  [per_device(): pl.pallas_call(functools.partial(kernel, s, tuple(scratch)), out_shape=(j...]
where the time goes in v4:
time: 125 us
  Pallas kernels  122 us (98%)
  local copies, waits for them, and re-layouts  1.8 us (1%)
    pallas_call x1, Pallas kernels, per_device(): pl.pallas_call(functools.partial(kernel, s, tuple(scratch)), out_shape=(j...  122 us

profile of v4, /device:TPU:1, one launch (start us, length us, event | category | flops | bytes accessed | tf_op | source)
XLA Modules:
  0.0 125.1 jit_solution(3935748265471589043)
XLA Ops:
  0.6 0.0 copy-start.2
  0.6 0.0 copy-start
  0.7 0.0 copy-start.1
  0.7 0.6 copy-done.2
  1.3 0.1 select_reduce_fusion
  1.4 0.0 copy-done.1
  1.4 0.0 copy-done
  1.5 122.5 %shard_map.50 = (bf16[64,1024]{1,0:T(8,128)(2,1)S(1)}, f32[1,128]{1,0:T(1,128)S(1)}) custom-call(bf16[32,1024]{1,0:T(8,128)(2,1)S(1)} %pad.4.emb, f32[1,256]{1,0:T(1,128)S(1)} %bitcast.5, s32[2,1024]{1,0:T(2,128)S(1)} %pad_add_fusion.qr_in, s32[1024]{0:T(1024)S(1)} %get-tuple-element.6.pos_in), custom_call_target="tpu_custom_call" | custom-call | tf_op jit(solution)/shard_map/pallas_call | solution.py:649
  124.0 0.5 slice_bitcast_fusion
  124.5 0.7 copy.6
  (4 shorter events, 0.1 us)
Async XLA Ops:
  0.6 0.7 copy-start.2
  0.6 0.8 copy-start
  0.7 0.7 copy-start.1

commit v5 on v4

--- a/solution.py
+++ b/solution.py
@@ -383,11 +383,11 @@
 
     def blocks(do):
         def step(b, carry):
-            do(2 * b)
-            do(2 * b + 1)
+            for i in range(4):
+                do(4 * b + i)
             return carry
 
-        lax.fori_loop(0, s.y // 2, step, 0)
+        lax.fori_loop(0, s.y // 4, step, 0)
 
     def lse_of(parts):
         top = functools.reduce(jnp.maximum, parts)

time: 125 us -> 125 us (level)
  no operation moved by 1% of the time
where the time goes in v5:
time: 125 us; the launch traced here: 124 us
  Pallas kernels  122 us (98%)
  local copies, waits for them, and re-layouts  1.8 us (1%)
    pallas_call x1, Pallas kernels, per_device(): pl.pallas_call(functools.partial(kernel, s, tuple(scratch)), out_shape=(j...  122 us

profile of v5, /device:TPU:1, one launch (start us, length us, event | category | flops | bytes accessed | tf_op | source)
XLA Modules:
  0.0 124.5 jit_solution(5446185043014703500)
XLA Ops:
  0.6 0.0 copy-start.2
  0.6 0.0 copy-start
  0.7 0.0 copy-start.1
  0.7 0.6 copy-done.2
  1.3 0.1 select_reduce_fusion
  1.4 0.0 copy-done.1
  1.4 0.0 copy-done
  1.5 121.8 %shard_map.50 = (bf16[64,1024]{1,0:T(8,128)(2,1)S(1)}, f32[1,128]{1,0:T(1,128)S(1)}) custom-call(bf16[32,1024]{1,0:T(8,128)(2,1)S(1)} %pad.4.emb, f32[1,256]{1,0:T(1,128)S(1)} %bitcast.5, s32[2,1024]{1,0:T(2,128)S(1)} %pad_add_fusion.qr_in, s32[1024]{0:T(1024)S(1)} %get-tuple-element.6.pos_in), custom_call_target="tpu_custom_call" | custom-call | tf_op jit(solution)/shard_map/pallas_call | solution.py:649
  123.3 0.5 slice_bitcast_fusion
  123.8 0.7 copy.6
  (4 shorter events, 0.1 us)
Async XLA Ops:
  0.6 0.7 copy-start.2
  0.6 0.8 copy-start
  0.7 0.7 copy-start.1
